TPU v7x, 32 devices: a whole 2x2x4 slice. The times are simulated.
32 devices in a mesh: groups: 2 (over y), vox: 4 (over z), sub: 2 (over x), map: 2 (over core).
Axes of the slice: x: 2, y: 2, z: 4, core: 2. Of those that a mesh axis runs over, the one named last changes fastest.
Arguments:
- data: bfloat16 [4, 256, 24576], P('groups', 'map', ('vox', 'sub')), parts along dimension 0, may hold values from -8 to 8
- maps: bfloat16 [400, 24576], P('groups', ('vox', 'sub')), parts along dimension 0, may hold values from -8 to 8
- neighbours: int32 [192, 4], P(('vox', 'sub')), may hold values from 0 to 191, as said below
- weights: float32 [4, 24576], P(None, ('vox', 'sub')), may hold values from 0.1 to 0.6
- noise_labels: int32 [128], P('groups'), parts along dimension 0, may hold values from 0 to 199, as said below
Outputs:
- clean: bfloat16 [4, 256, 24576], P('groups', 'map', ('vox', 'sub')), parts along dimension 0
There are 2 independent parts, one for each index of `groups`. A program takes and returns all parts, laid end to end along the dimension named above; an argument that names none is the same for every part. Nothing has to cross between parts.
Inputs may be any that keep to these rules, and one draw needn't show every extreme that they name: `neighbours`: every entry is within 1 of its own block index; each block lists one neighbour 1 above and one 1 below, cut at the ends of the voxel range. `noise_labels`: distinct component indices.
All inputs are finite; a program needn't handle non-finite values.
Results may differ from a plain program's by a relative error of at most 0.0008.
The roundings to bfloat16 on the way count: a program that leaves them out, or rounds other values in their place, can miss the bound.
Values may be sent and summed in bfloat16 or wider, within the bound.
A program may use at most 64 MiB of HBM per device.

v0:
```python
import jax
import jax.numpy as jnp
from jax import lax
from jax.sharding import PartitionSpec as P

VOXBLK = 128
NEIGHBOUR_REACH = 1


def padded(block, sides, width):
    for axis, dim in sides:
        count = lax.axis_size(axis)
        forward = [(i, i + 1) for i in range(count - 1)]
        backward = [(target, source) for source, target in forward]
        low = lax.ppermute(
            lax.slice_in_dim(block, block.shape[dim] - width, None, axis=dim), axis, forward
        )
        high = lax.ppermute(lax.slice_in_dim(block, 0, width, axis=dim), axis, backward)
        block = jnp.concatenate([low, block, high], axis=dim)
    return block


def solve_gram(gram, rhs):
    lower = jnp.linalg.cholesky(gram)
    half = lax.linalg.triangular_solve(lower, rhs, left_side=True, lower=True)
    return lax.linalg.triangular_solve(lower, half, left_side=True, lower=True, transpose_a=True)


def local(data, maps, neighbours, weights, noise_labels):
    subjects, frames, width = data.shape
    blocks = width // VOXBLK
    extended = padded(data, ((("vox", "sub"), 2),), NEIGHBOUR_REACH * VOXBLK)
    extended = extended.reshape(subjects, frames, blocks + 2 * NEIGHBOUR_REACH, VOXBLK)
    first_block = lax.axis_index(("vox", "sub")) * blocks - NEIGHBOUR_REACH
    local_index = neighbours - first_block
    slot_weights = weights.reshape(weights.shape[0], blocks, VOXBLK)
    total = data.astype(jnp.float32).reshape(subjects, frames, blocks, VOXBLK)
    for neighbour_slot in range(weights.shape[0]):
        picked = jnp.take(extended, local_index[:, neighbour_slot], axis=2)
        total = total + slot_weights[neighbour_slot] * picked.astype(jnp.float32)
    smoothed = total.reshape(subjects * frames, width).astype(jnp.bfloat16)
    gram_part = jnp.dot(maps, maps.T, preferred_element_type=jnp.float32)
    noise_maps = jnp.take(maps, noise_labels, axis=0)
    projection_part = jnp.einsum("cv,rv->cr", maps, smoothed, preferred_element_type=jnp.float32)
    gram, proj = lax.psum((gram_part, projection_part), ("vox", "sub"))
    beta = solve_gram(gram, proj)
    noise_beta = jnp.take(beta, noise_labels, axis=0).astype(jnp.bfloat16)
    fitted = jnp.einsum("kr,kv->rv", noise_beta, noise_maps, preferred_element_type=jnp.float32)
    clean = (smoothed.astype(jnp.float32) - fitted).astype(jnp.bfloat16)
    return clean.reshape(subjects, frames, width)


def solution(mesh):
    return jax.shard_map(
        local,
        mesh=mesh,
        in_specs=(
            P("groups", "map", ("vox", "sub")),
            P("groups", ("vox", "sub")),
            P(("vox", "sub"), None),
            P(None, ("vox", "sub")),
            P("groups"),
        ),
        out_specs=P("groups", "map", ("vox", "sub")),
        check_vma=False,
    )
```

profile of v0, /device:TPU:0, one launch (start us, length us, event | category | flops | bytes accessed | tf_op | source)
XLA Modules:
  0.0 183.6 jit_solution(4839692375885707667)
XLA Ops:
  6.5 2.0 %copy.18 = bf16[2,128,3072]{1,2,0:T(8,128)(2,1)S(1)} copy(bf16[2,128,3072]{2,1,0:T(8,128)(2,1)} %param.7) | data formatting | bytes 3145728 | tf_op args[0]
  8.6 4.8 %collective-permute-start = (bf16[2,128,128]{1,2,0:T(8,128)(2,1)S(1)}, bf16[2,128,128]{1,2,0:T(8,128)(2,1)S(1)}, u32[]{:S(2)}, u32[]{:S(2)}) collective-permute-start(bf16[2,128,128]{1,2,0:T(8,128)(2,1)S(1)} %get-tuple-element.36), channel_id=1, source_target_pairs={{0,2},{2,4},{4,6},{6,8},{8,10},{10,12},{12,14},{1,3},{3,5},{5,7},{... | collective-permute-start | bytes 196616 | tf_op jit(solution)/shard_map/ppermute | solution.py:15
  13.4 1.3 collective-permute-start.1
  14.8 2.1 %copy.23 = f32[2,128,24,128]{3,1,0,2:T(8,128)} copy(bf16[2,128,24,128]{1,3,2,0:T(8,128)(2,1)S(1)} %bitcast.71) | data formatting | bytes 4718592 | tf_op jit(solution)/shard_map/reshape | solution.py:37
  16.9 1.2 fusion.28
  18.2 1.4 collective-permute-done.1
  19.6 1.3 pad_maximum_fusion
  20.9 2.9 %copy.22 = bf16[2,128,26,128]{3,1,2,0:T(8,128)(2,1)S(1)} copy(bf16[2,128,26,128]{1,3,2,0:T(8,128)(2,1)} %bitcast.72) | data formatting | bytes 3407872 | tf_op jit(solution)/shard_map/reshape | solution.py:33
  23.8 1.9 %gather_fusion.2 = bf16[24,2,128,128]{3,2,1,0:T(8,128)(2,1)} fusion(bf16[2,128,26,128]{3,1,2,0:T(8,128)(2,1)S(1)} %copy.22, s32[1024]{0:T(1024)S(1)} %get-tuple-element.57), kind=kCustom, calls=%fused_computation.clone | custom fusion | bytes 3145824 | tf_op jit(solution)/shard_map/jit(_take)/gather | solution.py:39
  25.8 2.0 %gather_fusion.3 = bf16[24,2,128,128]{3,2,1,0:T(8,128)(2,1)} fusion(bf16[2,128,26,128]{3,1,2,0:T(8,128)(2,1)S(1)} %copy.22, s32[1024]{0:T(1024)S(1)} %get-tuple-element.56), kind=kCustom, calls=%fused_computation.1.clone | custom fusion | bytes 3145824 | tf_op jit(solution)/shard_map/jit(_take)/gather | solution.py:39
  27.7 2.0 %gather_fusion.4 = bf16[24,2,128,128]{3,2,1,0:T(8,128)(2,1)} fusion(bf16[2,128,26,128]{3,1,2,0:T(8,128)(2,1)S(1)} %copy.22, s32[1024]{0:T(1024)S(1)} %get-tuple-element.55), kind=kCustom, calls=%fused_computation.2.clone | custom fusion | bytes 3145824 | tf_op jit(solution)/shard_map/jit(_take)/gather | solution.py:39
  29.7 1.9 %gather_fusion.5 = bf16[24,2,128,128]{3,2,1,0:T(8,128)(2,1)} fusion(bf16[2,128,26,128]{3,1,2,0:T(8,128)(2,1)S(1)} %copy.22, s32[1024]{0:T(1024)S(1)} %get-tuple-element.54), kind=kCustom, calls=%fused_computation.3.clone | custom fusion | bytes 3145824 | tf_op jit(solution)/shard_map/jit(_take)/gather | solution.py:39
  31.6 5.3 %add_convert_fusion = bf16[2,128,24,128]{3,1,0,2:T(8,128)(2,1)S(1)} fusion(f32[2,128,24,128]{3,1,0,2:T(8,128)} %copy.23, bf16[24,2,128,128]{3,2,1,0:T(8,128)(2,1)} %gather_fusion.5, bf16[24,2,128,128]{3,2,1,0:T(8,128)(2,1)} %gather_fusion.4, bf16[24,2,128,128]{3,2,1,0:T(8,128)(2,1)} %gather_fusion.3, bf16[24,2,128,128]{3,2,1,0:T(8,128)(2,1)} %gather_fusion.2, ...), kind=kLoop, calls=%fused_computation.8 | loop fusion | flops 13369344 | bytes 11059296 | tf_op jit(solution)/shard_map/convert_element_type | solution.py:41
  38.0 1.3 fusion.4
  40.2 72.3 %all-reduce.6.cloned.1.call-done = (f32[200,256]{1,0:T(8,128)}, f32[200,200]{0,1:T(8,128)}) async-done(((f32[200,256]{1,0:T(8,128)}, f32[200,200]{0,1:T(8,128)}), (f32[200,256]{1,0:T(8,128)}, f32[200,200]{0,1:T(8,128)})) %all-reduce.6.cloned.1.call-update) | async-done | bytes 364816 | tf_op jit(solution)/shard_map/psum | solution.py:45
  112.5 1.0 copy.29
  115.2 11.7 %cholesky.51 = f32[128,128]{1,0:T(8,128)S(1)} custom-call(f32[128,128]{1,0:T(8,128)S(1)} %cholesky.124), custom_call_target="Cholesky" | custom-call | tf_op jit(solution)/shard_map/jit(cholesky)/cholesky | solution.py:24
  127.6 10.6 %custom-call.16 = f32[1,128,128]{1,2,0:T(8,128)S(1)} custom-call(f32[1,128,128]{2,1,0:T(8,128)} %get-tuple-element.39), custom_call_target="InvertDiagBlocksLowerTriangular" | custom-call | tf_op jit(solution)/shard_map/jit(cholesky)/cholesky | solution.py:24
  140.2 6.6 %cholesky.110 = f32[72,72]{1,0:T(8,128)S(1)} custom-call(f32[72,72]{1,0:T(8,128)S(1)} %convolution_subtract_fusion.3), custom_call_target="Cholesky" | custom-call | tf_op jit(solution)/shard_map/jit(cholesky)/cholesky | solution.py:24
  150.3 19.7 %custom-call.17 = f32[2,128,128]{1,2,0:T(8,128)S(1)} custom-call(f32[2,128,128]{2,1,0:T(8,128)S(1)} %pad_maximum_fusion.2), custom_call_target="InvertDiagBlocksLowerTriangular" | custom-call | tf_op jit(solution)/shard_map/triangular_solve | solution.py:26
  170.0 1.2 fusion.11
  171.2 1.1 convolution_subtract_fusion.2
  172.8 1.1 convolution_subtract_fusion.1
  174.9 1.8 fusion
  (47 shorter events, 9.8 us)
Async XLA Ops:
  6.5 10.4 %copy-start = (bf16[200,3072]{1,0:T(8,128)(2,1)S(1)}, bf16[200,3072]{1,0:T(8,128)(2,1)}, u32[]{:S(2)}) copy-start(bf16[200,3072]{1,0:T(8,128)(2,1)} %param.8) | copy-start | bytes 3686404
  6.5 8.2 %copy-start.4 = (s32[24,4]{0,1:T(4,128)S(1)}, s32[24,4]{0,1:T(4,128)}, u32[]{:S(2)}) copy-start(s32[24,4]{0,1:T(4,128)} %param.9) | copy-start | bytes 1156
  6.5 8.2 %copy-start.3 = (f32[4,3072]{1,0:T(4,128)S(1)}, f32[4,3072]{1,0:T(4,128)}, u32[]{:S(2)}) copy-start(f32[4,3072]{1,0:T(4,128)} %param.10) | copy-start | bytes 147460
  6.5 106.0 %all-reduce.6.cloned.1.call-start = ((), (), s32[]{:S(2)}) async-start(), calls=%async_computation | async-start | bytes 819200 | tf_op jit(solution)/shard_map/psum | solution.py:45
  8.6 9.6 %collective-permute-start = (bf16[2,128,128]{1,2,0:T(8,128)(2,1)S(1)}, bf16[2,128,128]{1,2,0:T(8,128)(2,1)S(1)}, u32[]{:S(2)}, u32[]{:S(2)}) collective-permute-start(bf16[2,128,128]{1,2,0:T(8,128)(2,1)S(1)} %get-tuple-element.36), channel_id=1, source_target_pairs={{0,2},{2,4},{4,6},{6,8},{8,10},{10,12},{12,14},{1,3},{3,5},{5,7},{... | collective-permute-start | bytes 196616 | tf_op jit(solution)/shard_map/ppermute | solution.py:15
  13.4 6.2 %collective-permute-start.1 = (bf16[2,128,128]{1,2,0:T(8,128)(2,1)S(1)}, bf16[2,128,128]{1,2,0:T(8,128)(2,1)S(1)}, u32[]{:S(2)}, u32[]{:S(2)}) collective-permute-start(bf16[2,128,128]{1,2,0:T(8,128)(2,1)S(1)} %get-tuple-element.37), channel_id=1, source_target_pairs={{2,0},{4,2},{6,4},{8,6},{10,8},{12,10},{14,12},{3,1},{5,3},{7,5},{... | collective-permute-start | bytes 196616 | tf_op jit(solution)/shard_map/ppermute | solution.py:18
  16.9 1.2 copy-start.5
  114.5 0.7 copy-start.2
  149.5 0.7 copy-start.1
Sparse Core Ops, SparseCore 0:
  39.4 73.0 all-reduce.5
where the time goes:
time: 184 us
  waiting for transfers between devices  73.8 us (40%)
  other arithmetic  58.4 us (32%)
  local copies, waits for them, and re-layouts  19.8 us (11%)
  between operations  15 us (8%)
  matrix products  10.5 us (6%)
  starting transfers between devices  6.14 us (3%)
    psum x1, waiting for transfers between devices, local(): gram, proj = lax.psum((gram_part, projection_part), ('vox', 'sub'))  72.3 us
    another operation x7, other arithmetic, solve_gram(): lower = jnp.linalg.cholesky(gram)  31 us
    another operation x7, other arithmetic, solve_gram(): lax.linalg.triangular_solve(lower, half, left_side=True, lower=True, tran...  19.8 us
    gather x4, local copies, waits for them, and re-layouts, local(): picked = jnp.take(extended, local_index[:, neighbour_slot], axis=2)  7.8 us
    convert_element_type x1, other arithmetic, local(): smoothed = total.reshape(subjects * frames, width).astype(jnp.bfloat16)  5.3 us
    ppermute x1, starting transfers between devices, padded(): lax.ppermute(lax.slice_in_dim(block, block.shape[dim] - width, None, axis...  4.85 us
  transfers between devices with their start and end apart: 3, of which 2 were waited for; matrix products, arithmetic and copies ran while one was open for 2% of the time, Pallas kernels for 0%

commit v1 on v0

v1 whole, which is shorter than its diff:
```python
import functools
import jax
import jax.numpy as jnp
from jax import lax
from jax.experimental import pallas as pl
from jax.experimental.pallas import tpu as pltpu
from jax.sharding import PartitionSpec as P

VOXBLK = 128
NEIGHBOUR_REACH = 1
MESH = pl.DeviceIdType.MESH
HIGHEST = lax.Precision.HIGHEST
NN = (((1,), (0,)), ((), ()))
NT = (((1,), (1,)), ((), ()))
TN = (((0,), (0,)), ((), ()))


def f32_dot(a, b, dims):
    return lax.dot_general(a, b, dims, precision=HIGHEST, preferred_element_type=jnp.float32)


def negative_inverse_small(block):
    size = block.shape[0]
    row_id = lax.broadcasted_iota(jnp.int32, (size, size), 0)
    col_id = lax.broadcasted_iota(jnp.int32, (size, size), 1)
    for k in range(size):
        pivot = block[k : k + 1, k : k + 1]
        row = jnp.where(col_id[:1] == k, -1.0, block[k : k + 1, :])
        col = jnp.where(row_id[:, :1] == k, -1.0, block[:, k : k + 1])
        rest = jnp.where((row_id == k) | (col_id == k), 0.0, block)
        block = rest - col * (row * (1.0 / pivot))
    return block


def negative_inverse(gram_ref, work_ref, size, step):
    row_id = lax.broadcasted_iota(jnp.int32, (size, size), 0)
    col_id = lax.broadcasted_iota(jnp.int32, (size, size), 1)
    own_row = lax.broadcasted_iota(jnp.int32, (step, size), 0)
    own_col = lax.broadcasted_iota(jnp.int32, (step, size), 1)
    work_ref[...] = gram_ref[pl.ds(0, size), :]
    for first in range(0, size, step):
        rows = work_ref[pl.ds(first, step), :]
        select = (own_col == own_row + first).astype(jnp.float32)
        small = negative_inverse_small(f32_dot(rows, select, NT))
        in_cols = (own_col >= first) & (own_col < first + step)
        turned = jnp.where(in_cols, -select, rows)
        update = f32_dot(turned, f32_dot(small, turned, NN), TN)
        inside = ((row_id >= first) & (row_id < first + step)) | (
            (col_id >= first) & (col_id < first + step)
        )
        work_ref[...] = jnp.where(inside, 0.0, work_ref[...]) + update


def kernel(
    count, sub_count, share, gram_share, step,
    data_ref, maps_ref, coef_ref, keep_ref,
    smooth_ref, beta_ref,
    low_ref, high_ref, gram_part, gram_in, gram_all, proj_part, proj_in, work_ref, beta_all,
    halo_send, halo_recv, gsend, grecv, asend, arecv, psend, precv, bsend, brecv,
):
    comps, width = maps_ref.shape
    blocks = width // VOXBLK
    me = lax.axis_index("vox") * sub_count + lax.axis_index("sub")

    def peer(k):
        return lax.rem(me + k, count)

    def device(index):
        return {"vox": lax.div(index, sub_count), "sub": lax.rem(index, sub_count)}

    def send(src, dst, send_sem, recv_sem, index):
        copy = pltpu.make_async_remote_copy(
            src_ref=src, dst_ref=dst, send_sem=send_sem, recv_sem=recv_sem,
            device_id=device(index), device_id_type=MESH,
        )
        copy.start()
        return copy

    def part(index, size, align):
        return pl.ds(pl.multiple_of(index * size, align), size)

    barrier = pltpu.get_barrier_semaphore()
    for k in range(1, count):
        pl.semaphore_signal(barrier, inc=1, device_id=device(peer(k)), device_id_type=MESH)
    pl.semaphore_wait(barrier, count - 1)

    halo = [
        send(data_ref.at[:, pl.ds(width - VOXBLK, VOXBLK)], low_ref,
             halo_send.at[0], halo_recv.at[0], peer(1)),
        send(data_ref.at[:, pl.ds(0, VOXBLK)], high_ref,
             halo_send.at[1], halo_recv.at[1], peer(count - 1)),
    ]

    maps = maps_ref[...]
    if gram_part.shape[0] > comps:
        gram_part[pl.ds(comps, gram_part.shape[0] - comps), :] = jnp.zeros(
            (gram_part.shape[0] - comps, comps), jnp.float32
        )
    gram_part[pl.ds(0, comps), :] = lax.dot_general(maps, maps, NT, preferred_element_type=jnp.float32)
    gram_copies = [
        send(gram_part.at[part(peer(k), gram_share, 8), :], gram_in.at[k], gsend.at[k], grecv.at[k], peer(k))
        for k in range(1, count)
    ]

    def columns(block):
        start = block * VOXBLK
        return pl.ds(start if isinstance(block, int) else pl.multiple_of(start, VOXBLK), VOXBLK)

    def smooth(block, low, high):
        here = columns(block)
        weight = coef_ref[:, here]
        total = data_ref[:, here].astype(jnp.float32) * weight[1:2]
        total = total + low.astype(jnp.float32) * weight[0:1] + high.astype(jnp.float32) * weight[2:3]
        smooth_ref[:, here] = total.astype(jnp.bfloat16)

    def inner(block, carry):
        smooth(block, data_ref[:, columns(block - 1)], data_ref[:, columns(block + 1)])
        return carry

    lax.fori_loop(1, blocks - 1, inner, 0)

    for copy in gram_copies:
        copy.wait()
    own = part(me, gram_share, 8)
    total = gram_part[own, :]
    for k in range(1, count):
        total = total + gram_in[k]
    gram_all[own, :] = total
    all_copies = [
        send(gram_all.at[own, :], gram_all.at[own, :], asend.at[k], arecv.at[k], peer(k))
        for k in range(1, count)
    ]

    for copy in halo:
        copy.wait()
    smooth(0, low_ref[...], data_ref[:, columns(1)])
    smooth(blocks - 1, data_ref[:, columns(blocks - 2)], high_ref[...])
    proj_part[...] = lax.dot_general(smooth_ref[...], maps, NT, preferred_element_type=jnp.float32)
    proj_copies = [
        send(proj_part.at[part(peer(k), share, 16), :], proj_in.at[k], psend.at[k], precv.at[k], peer(k))
        for k in range(1, count)
    ]

    for copy in all_copies:
        copy.wait()
    negative_inverse(gram_all, work_ref, comps, step)

    for copy in proj_copies:
        copy.wait()
    mine = part(me, share, 16)
    rhs = proj_part[mine, :]
    for k in range(1, count):
        rhs = rhs + proj_in[k]
    gram = gram_all[pl.ds(0, comps), :]
    beta = -f32_dot(rhs, work_ref[...], NN)
    left = rhs - f32_dot(beta, gram, NN)
    beta = beta - f32_dot(left, work_ref[...], NN)
    beta_all[mine, :] = jnp.where(keep_ref[...] > 0.0, beta, 0.0).astype(jnp.bfloat16)
    beta_copies = [
        send(beta_all.at[mine, :], beta_all.at[mine, :], bsend.at[k], brecv.at[k], peer(k))
        for k in range(1, count)
    ]
    for copy in beta_copies:
        copy.wait()
    beta_ref[...] = beta_all[...]


def fused(frames, maps, coef, keep, count, sub_count):
    rows, width = frames.shape
    comps = maps.shape[0]
    share = rows // count
    gram_share = 8 * (-(-comps // (8 * count)))
    step = next(size for size in (40, 32, 24, 16, 8) if comps % size == 0)
    f32, bf16 = jnp.float32, jnp.bfloat16
    vmem = pl.BlockSpec(memory_space=pltpu.VMEM)
    sems = pltpu.SemaphoreType.DMA((count,))
    return pl.pallas_call(
        functools.partial(kernel, count, sub_count, share, gram_share, step),
        out_shape=(
            jax.ShapeDtypeStruct((rows, width), bf16),
            jax.ShapeDtypeStruct((rows, comps), bf16),
        ),
        in_specs=[vmem] * 4,
        out_specs=(vmem, vmem),
        scratch_shapes=[
            pltpu.VMEM((rows, VOXBLK), bf16),
            pltpu.VMEM((rows, VOXBLK), bf16),
            pltpu.VMEM((count * gram_share, comps), f32),
            pltpu.VMEM((count, gram_share, comps), f32),
            pltpu.VMEM((count * gram_share, comps), f32),
            pltpu.VMEM((rows, comps), f32),
            pltpu.VMEM((count, share, comps), f32),
            pltpu.VMEM((comps, comps), f32),
            pltpu.VMEM((rows, comps), bf16),
            pltpu.SemaphoreType.DMA((2,)),
            pltpu.SemaphoreType.DMA((2,)),
            sems, sems, sems, sems, sems, sems, sems, sems,
        ],
        compiler_params=pltpu.CompilerParams(
            collective_id=0, has_side_effects=True, vmem_limit_bytes=48 * 1024 * 1024
        ),
    )(frames, maps, coef, keep)


def solve_gram(gram, rhs):
    lower = jnp.linalg.cholesky(gram)
    half = lax.linalg.triangular_solve(lower, rhs, left_side=True, lower=True)
    return lax.linalg.triangular_solve(lower, half, left_side=True, lower=True, transpose_a=True)


def by_collectives(frames, maps, coef, keep, count):
    forward = [(i, (i + 1) % count) for i in range(count)]
    backward = [(target, source) for source, target in forward]
    low = lax.ppermute(frames[:, -VOXBLK:], ("vox", "sub"), forward)
    high = lax.ppermute(frames[:, :VOXBLK], ("vox", "sub"), backward)
    below = jnp.concatenate([low, frames[:, :-VOXBLK]], axis=1).astype(jnp.float32)
    above = jnp.concatenate([frames[:, VOXBLK:], high], axis=1).astype(jnp.float32)
    smoothed = frames.astype(jnp.float32) * coef[1:2] + below * coef[0:1] + above * coef[2:3]
    smoothed = smoothed.astype(jnp.bfloat16)
    gram = lax.dot_general(maps, maps, NT, preferred_element_type=jnp.float32)
    proj = lax.dot_general(maps, smoothed, NT, preferred_element_type=jnp.float32)
    gram, proj = lax.psum((gram, proj), ("vox", "sub"))
    beta = solve_gram(gram, proj).T
    return smoothed, jnp.where(keep > 0.0, beta, 0.0).astype(jnp.bfloat16)


def local(data, maps, neighbours, weights, noise_labels):
    subjects, frames, width = data.shape
    comps = maps.shape[0]
    blocks = width // VOXBLK
    rows = subjects * frames
    sub_count = lax.axis_size("sub")
    count = lax.axis_size("vox") * sub_count
    own = lax.axis_index(("vox", "sub")) * blocks + jnp.arange(blocks, dtype=jnp.int32)
    offset = (neighbours - own[:, None]).T[:, :, None]
    slots = weights.reshape(weights.shape[0], blocks, VOXBLK)
    coef = jnp.stack(
        [
            jnp.sum(jnp.where(offset == reach, slots, 0.0), axis=0) + (1.0 if reach == 0 else 0.0)
            for reach in range(-NEIGHBOUR_REACH, NEIGHBOUR_REACH + 1)
        ]
    ).reshape(2 * NEIGHBOUR_REACH + 1, width)
    labels = lax.broadcasted_iota(jnp.int32, (noise_labels.shape[0], comps), 1)
    keep = jnp.max((labels == noise_labels[:, None]).astype(jnp.float32), axis=0, keepdims=True)
    stacked = data.reshape(rows, width)
    if rows % (16 * count) == 0 and count <= 16 and blocks > 2:
        smoothed, beta = fused(stacked, maps, coef, keep, count, sub_count)
    else:
        smoothed, beta = by_collectives(stacked, maps, coef, keep, count)
    fitted = jnp.einsum("rc,cv->rv", beta, maps, preferred_element_type=jnp.float32)
    clean = (smoothed.astype(jnp.float32) - fitted).astype(jnp.bfloat16)
    return clean.reshape(subjects, frames, width)


def solution(mesh):
    return jax.shard_map(
        local,
        mesh=mesh,
        in_specs=(
            P("groups", "map", ("vox", "sub")),
            P("groups", ("vox", "sub")),
            P(("vox", "sub"), None),
            P(None, ("vox", "sub")),
            P("groups"),
        ),
        out_specs=P("groups", "map", ("vox", "sub")),
        check_vma=False,
    )
```

time: 184 us -> 58.4 us (0.32)
  waiting for transfers between devices: 73.8 us -> 0 us
  other arithmetic: 58.4 us -> 2.4 us
  Pallas kernels: 0 us -> 51.1 us
  local copies, waits for them, and re-layouts: 19.8 us -> 2.86 us
  between operations: 15 us -> 0.05 us
  matrix products: 10.5 us -> 1.74 us
  starting transfers between devices: 6.14 us -> 0 us
    psum x1 -> x0, waiting for transfers between devices: 72.3 us -> none  [local(): gram, proj = lax.psum((gram_part, projection_part), ('vox', 'sub'))]
    pallas_call x0 -> x1, Pallas kernels: none -> 51.1 us  [fused(): pl.pallas_call(functools.partial(kernel, count, sub_count, share, gram_sh...]
    another operation x14 -> x1, other arithmetic: 50.8 us -> 0.04 us  [local(): jnp.stack([jnp.sum(jnp.where(offset == reach, slots, 0.0), axis=0) + (1.0...]
    gather x6 -> x0, local copies, waits for them, and re-layouts: 9.28 us -> none  [the longest x4 7.8 us: local(): picked = jnp.take(extended, local_index[:, neighbour_slot], axis=2)]
    ppermute x2 -> x0, starting transfers between devices: 6.14 us -> none  [the longest x1 4.85 us: padded(): lax.ppermute(lax.slice_in_dim(block, block.shape[dim] - width, None, axis...]
    another operation x8 -> x0, matrix products: 6.09 us -> none  [the longest x3 2.59 us: solve_gram(): half = lax.linalg.triangular_solve(lower, rhs, left_side=True, lower=True)]
    convert_element_type x1 -> x0, other arithmetic: 5.3 us -> none  [local(): smoothed = total.reshape(subjects * frames, width).astype(jnp.bfloat16)]
    reshape x2 -> x0, local copies, waits for them, and re-layouts: 4.98 us -> none  [the longest x1 2.92 us: local(): extended.reshape(subjects, frames, blocks + 2 * NEIGHBOUR_REACH, VOXBLK)]
  transfers between devices with their start and end apart: 3 -> 0, of which waited for: 2 -> 0; matrix products, arithmetic and copies ran while one was open for 2% -> 0% of each run, Pallas kernels for 0% -> 0%
where the time goes in v1:
time: 58.4 us; the launch traced here: 58.2 us
  Pallas kernels  51.1 us (88%)
  local copies, waits for them, and re-layouts  2.86 us (5%)
  other arithmetic  2.4 us (4%)
  matrix products  1.74 us (3%)
    pallas_call x1, Pallas kernels, fused(): pl.pallas_call(functools.partial(kernel, count, sub_count, share, gram_sh...  51.1 us
    unnamed x6, local copies, waits for them, and re-layouts  2.86 us
    dot_general x1, matrix products, local(): jnp.einsum('rc,cv->rv', beta, maps, preferred_element_type=jnp.float32)  1.74 us

profile of v1, /device:TPU:0, one launch (start us, length us, event | category | flops | bytes accessed | tf_op | source)
XLA Modules:
  0.0 58.2 jit_solution(9472434370302130477)
XLA Ops:
  0.0 0.7 %convert_reduce_fusion = f32[200]{0:T(256)S(1)} fusion(s32[64]{0:T(128)} %param.9), kind=kLoop, calls=%fused_computation.2 | loop fusion | flops 38200 | bytes 1056 | tf_op jit(solution)/shard_map/reduce_max | solution.py:244
  0.8 0.7 %compare_bitcast_fusion.1 = (pred[4,24]{1,0:T(4,128)(4,1)S(1)}, pred[4,24]{1,0:T(4,128)(4,1)S(1)}, pred[4,24]{1,0:T(4,128)(4,1)S(1)}) fusion(s32[24,4]{0,1:T(4,128)} %param.7, s32[24]{0:T(128)S(1)} %iota_add_fusion), kind=kLoop, calls=%fused_computation.13 | loop fusion | flops 384 | bytes 768 | tf_op jit(solution)/shard_map/eq | solution.py:239
  1.4 0.1 broadcast_bitcast_fusion.2
  1.5 0.1 broadcast_bitcast_fusion
  1.6 0.9 %select_reduce_fusion.2 = (f32[3072]{0:T(1024)S(1)}, f32[3072]{0:T(1024)S(1)}, f32[3072]{0:T(1024)S(1)}) fusion(f32[4,3072]{1,0:T(4,128)} %param.8, pred[1,4,24,128]{3,2,1,0:T(8,128)(4,1)S(1)} %broadcast_bitcast_fusion.2, pred[1,4,24,128]{3,2,1,0:T(8,128)(4,1)S(1)} %get-tuple-element.15, pred[1,4,24,128]{3,2,1,0:T(8,128)(4,1)S(1)} %get-tuple-element.16), kind=kLoop, calls=%fused_computation.7 | loop fusion | flops 64512 | bytes 122880 | tf_op jit(solution)/shard_map/reduce_sum | solution.py:239
  2.6 0.0 copy-start
  2.6 1.3 %copy-done = bf16[200,3072]{1,0:T(8,128)(2,1)S(1)} copy-done((bf16[200,3072]{1,0:T(8,128)(2,1)S(1)}, bf16[200,3072]{1,0:T(8,128)(2,1)}, u32[]{:S(2)}) %copy-start) | copy-done | bytes 1228824
  3.9 0.0 copy-start.1
  3.9 1.4 %copy-done.1 = bf16[2,128,3072]{2,1,0:T(8,128)(2,1)S(1)} copy-done((bf16[2,128,3072]{2,1,0:T(8,128)(2,1)S(1)}, bf16[2,128,3072]{2,1,0:T(8,128)(2,1)}, u32[]{:S(2)}) %copy-start.1) | copy-done | bytes 1572888
  5.3 51.1 %shard_map.55 = (bf16[256,3072]{1,0:T(8,128)(2,1)S(1)}, bf16[256,200]{1,0:T(8,128)(2,1)S(1)}) custom-call(bf16[256,3072]{1,0:T(8,128)(2,1)S(1)} %bitcast.26, bf16[200,3072]{1,0:T(8,128)(2,1)S(1)} %copy-done, f32[3,3072]{1,0:T(4,128)S(1)} %pad_maximum_fusion.coef_ref, f32[1,200]{1,0:T(1,128)S(1)} %bitcast.27), custom_call_target="tpu_custom_call" | custom-call | tf_op jit(solution)/shard_map/pallas_call | solution.py:177
  56.4 1.7 %fusion = bf16[256,3072]{1,0:T(8,128)(2,1)} fusion(bf16[256,200]{1,0:T(8,128)(2,1)S(1)} %get-tuple-element.8, bf16[200,3072]{1,0:T(8,128)(2,1)S(1)} %copy-done, bf16[256,3072]{1,0:T(8,128)(2,1)S(1)} %get-tuple-element.7), kind=kOutput, calls=%fused_computation.1 | convolution fusion | flops 316932096 | bytes 4476928 | tf_op jit(solution)/shard_map/rc,cv->rv/dot_general | solution.py:250
  (3 shorter events, 0.0 us)
Async XLA Ops:
  2.6 1.3 %copy-start = (bf16[200,3072]{1,0:T(8,128)(2,1)S(1)}, bf16[200,3072]{1,0:T(8,128)(2,1)}, u32[]{:S(2)}) copy-start(bf16[200,3072]{1,0:T(8,128)(2,1)} %maps_ref.1) | copy-start | bytes 3686404
  3.9 1.4 %copy-start.1 = (bf16[2,128,3072]{2,1,0:T(8,128)(2,1)S(1)}, bf16[2,128,3072]{2,1,0:T(8,128)(2,1)}, u32[]{:S(2)}) copy-start(bf16[2,128,3072]{2,1,0:T(8,128)(2,1)} %param.5) | copy-start | bytes 4718596

commit v2 on v1

--- a/solution.py
+++ b/solution.py
@@ -8,6 +8,7 @@
 
 VOXBLK = 128
 NEIGHBOUR_REACH = 1
+PIVOTS = 8
 MESH = pl.DeviceIdType.MESH
 HIGHEST = lax.Precision.HIGHEST
 NN = (((1,), (0,)), ((), ()))
@@ -19,16 +20,50 @@
     return lax.dot_general(a, b, dims, precision=HIGHEST, preferred_element_type=jnp.float32)
 
 
+def swept(entries, size):
+    def at(i, j):
+        return entries[(min(i, j), max(i, j))]
+
+    for p in range(size):
+        inverse = 1.0 / at(p, p)
+        scaled = {i: at(i, p) * inverse for i in range(size) if i != p}
+        later = {}
+        for i in range(size):
+            for j in range(i, size):
+                if i == p and j == p:
+                    later[(i, j)] = -inverse
+                elif i == p:
+                    later[(i, j)] = scaled[j]
+                elif j == p:
+                    later[(i, j)] = scaled[i]
+                else:
+                    later[(i, j)] = at(i, j) - at(i, p) * scaled[j]
+        entries = later
+    return entries
+
+
 def negative_inverse_small(block):
     size = block.shape[0]
     row_id = lax.broadcasted_iota(jnp.int32, (size, size), 0)
     col_id = lax.broadcasted_iota(jnp.int32, (size, size), 1)
-    for k in range(size):
-        pivot = block[k : k + 1, k : k + 1]
-        row = jnp.where(col_id[:1] == k, -1.0, block[k : k + 1, :])
-        col = jnp.where(row_id[:, :1] == k, -1.0, block[:, k : k + 1])
-        rest = jnp.where((row_id == k) | (col_id == k), 0.0, block)
-        block = rest - col * (row * (1.0 / pivot))
+    for first in range(0, size, PIVOTS):
+        group = range(PIVOTS)
+        cols = [jnp.broadcast_to(block[:, first + j : first + j + 1], (size, size)) for j in group]
+        rows = [block[first + i : first + i + 1, :] for i in group]
+        upper = {(i, j): cols[j][first + i : first + i + 1, :] for i in group for j in group if i <= j}
+        pivots = swept(upper, PIVOTS)
+        in_rows = (row_id >= first) & (row_id < first + PIVOTS)
+        in_cols = (col_id >= first) & (col_id < first + PIVOTS)
+        rows = [
+            jnp.where(col_id[:1] == first + i, -1.0, jnp.where(in_cols[:1], 0.0, rows[i])) for i in group
+        ]
+        cols = [jnp.where(row_id == first + i, -1.0, jnp.where(in_rows, 0.0, cols[i])) for i in group]
+        block = jnp.where(in_rows | in_cols, 0.0, block)
+        for i in group:
+            mixed = pivots[(0, i)] * rows[0]
+            for j in group[1:]:
+                mixed = mixed + pivots[(min(i, j), max(i, j))] * rows[j]
+            block = block + cols[i] * mixed
     return block
 
 
@@ -41,7 +76,7 @@
     for first in range(0, size, step):
         rows = work_ref[pl.ds(first, step), :]
         select = (own_col == own_row + first).astype(jnp.float32)
-        small = negative_inverse_small(f32_dot(rows, select, NT))
+        small = negative_inverse_small(rows[:, first : first + step])
         in_cols = (own_col >= first) & (own_col < first + step)
         turned = jnp.where(in_cols, -select, rows)
         update = f32_dot(turned, f32_dot(small, turned, NN), TN)

time: 58.4 us -> 47.2 us (0.81)
  Pallas kernels: 51.1 us -> 39.8 us
    pallas_call x1, Pallas kernels: 51.1 us -> 39.8 us  [fused(): pl.pallas_call(functools.partial(kernel, count, sub_count, share, gram_sh...]
where the time goes in v2:
time: 47.2 us; the launch traced here: 46.9 us
  Pallas kernels  39.8 us (84%)
  local copies, waits for them, and re-layouts  2.86 us (6%)
  other arithmetic  2.4 us (5%)
  matrix products  1.74 us (4%)
    pallas_call x1, Pallas kernels, fused(): pl.pallas_call(functools.partial(kernel, count, sub_count, share, gram_sh...  39.8 us
    unnamed x6, local copies, waits for them, and re-layouts  2.86 us
    dot_general x1, matrix products, local(): jnp.einsum('rc,cv->rv', beta, maps, preferred_element_type=jnp.float32)  1.74 us

profile of v2, /device:TPU:0, one launch (start us, length us, event | category | flops | bytes accessed | tf_op | source)
XLA Modules:
  0.0 46.9 jit_solution(15693015510578659874)
XLA Ops:
  0.0 0.7 %convert_reduce_fusion = f32[200]{0:T(256)S(1)} fusion(s32[64]{0:T(128)} %param.9), kind=kLoop, calls=%fused_computation.2 | loop fusion | flops 38200 | bytes 1056 | tf_op jit(solution)/shard_map/reduce_max | solution.py:279
  0.8 0.7 %compare_bitcast_fusion.1 = (pred[4,24]{1,0:T(4,128)(4,1)S(1)}, pred[4,24]{1,0:T(4,128)(4,1)S(1)}, pred[4,24]{1,0:T(4,128)(4,1)S(1)}) fusion(s32[24,4]{0,1:T(4,128)} %param.7, s32[24]{0:T(128)S(1)} %iota_add_fusion), kind=kLoop, calls=%fused_computation.13 | loop fusion | flops 384 | bytes 768 | tf_op jit(solution)/shard_map/eq | solution.py:274
  1.4 0.1 broadcast_bitcast_fusion.2
  1.5 0.1 broadcast_bitcast_fusion
  1.6 0.9 %select_reduce_fusion.2 = (f32[3072]{0:T(1024)S(1)}, f32[3072]{0:T(1024)S(1)}, f32[3072]{0:T(1024)S(1)}) fusion(f32[4,3072]{1,0:T(4,128)} %param.8, pred[1,4,24,128]{3,2,1,0:T(8,128)(4,1)S(1)} %broadcast_bitcast_fusion.2, pred[1,4,24,128]{3,2,1,0:T(8,128)(4,1)S(1)} %get-tuple-element.15, pred[1,4,24,128]{3,2,1,0:T(8,128)(4,1)S(1)} %get-tuple-element.16), kind=kLoop, calls=%fused_computation.7 | loop fusion | flops 64512 | bytes 122880 | tf_op jit(solution)/shard_map/reduce_sum | solution.py:274
  2.6 0.0 copy-start
  2.6 1.3 %copy-done = bf16[200,3072]{1,0:T(8,128)(2,1)S(1)} copy-done((bf16[200,3072]{1,0:T(8,128)(2,1)S(1)}, bf16[200,3072]{1,0:T(8,128)(2,1)}, u32[]{:S(2)}) %copy-start) | copy-done | bytes 1228824
  3.9 0.0 copy-start.1
  3.9 1.4 %copy-done.1 = bf16[2,128,3072]{2,1,0:T(8,128)(2,1)S(1)} copy-done((bf16[2,128,3072]{2,1,0:T(8,128)(2,1)S(1)}, bf16[2,128,3072]{2,1,0:T(8,128)(2,1)}, u32[]{:S(2)}) %copy-start.1) | copy-done | bytes 1572888
  5.3 39.8 %shard_map.55 = (bf16[256,3072]{1,0:T(8,128)(2,1)S(1)}, bf16[256,200]{1,0:T(8,128)(2,1)S(1)}) custom-call(bf16[256,3072]{1,0:T(8,128)(2,1)S(1)} %bitcast.26, bf16[200,3072]{1,0:T(8,128)(2,1)S(1)} %copy-done, f32[3,3072]{1,0:T(4,128)S(1)} %pad_maximum_fusion.coef_ref, f32[1,200]{1,0:T(1,128)S(1)} %bitcast.27), custom_call_target="tpu_custom_call" | custom-call | tf_op jit(solution)/shard_map/pallas_call | solution.py:212
  45.2 1.7 %fusion = bf16[256,3072]{1,0:T(8,128)(2,1)} fusion(bf16[256,200]{1,0:T(8,128)(2,1)S(1)} %get-tuple-element.8, bf16[200,3072]{1,0:T(8,128)(2,1)S(1)} %copy-done, bf16[256,3072]{1,0:T(8,128)(2,1)S(1)} %get-tuple-element.7), kind=kOutput, calls=%fused_computation.1 | convolution fusion | flops 316932096 | bytes 4476928 | tf_op jit(solution)/shard_map/rc,cv->rv/dot_general | solution.py:285
  (3 shorter events, 0.0 us)
Async XLA Ops:
  2.6 1.3 %copy-start = (bf16[200,3072]{1,0:T(8,128)(2,1)S(1)}, bf16[200,3072]{1,0:T(8,128)(2,1)}, u32[]{:S(2)}) copy-start(bf16[200,3072]{1,0:T(8,128)(2,1)} %maps_ref.1) | copy-start | bytes 3686404
  3.9 1.4 %copy-start.1 = (bf16[2,128,3072]{2,1,0:T(8,128)(2,1)S(1)}, bf16[2,128,3072]{2,1,0:T(8,128)(2,1)}, u32[]{:S(2)}) copy-start(bf16[2,128,3072]{2,1,0:T(8,128)(2,1)} %param.5) | copy-start | bytes 4718596

commit v3 on v2

--- a/solution.py
+++ b/solution.py
@@ -88,8 +88,9 @@
 
 def kernel(
     count, sub_count, share, gram_share, step,
-    data_ref, maps_ref, coef_ref, keep_ref,
+    data_hbm, maps_hbm, coef_ref, keep_ref,
     smooth_ref, beta_ref,
+    data_ref, maps_ref, load_sems,
     low_ref, high_ref, gram_part, gram_in, gram_all, proj_part, proj_in, work_ref, beta_all,
     halo_send, halo_recv, gsend, grecv, asend, arecv, psend, precv, bsend, brecv,
 ):
@@ -114,18 +115,17 @@
     def part(index, size, align):
         return pl.ds(pl.multiple_of(index * size, align), size)
 
+    load_maps = pltpu.make_async_copy(maps_hbm, maps_ref, load_sems.at[0])
+    load_data = pltpu.make_async_copy(data_hbm, data_ref, load_sems.at[1])
+    load_maps.start()
+    load_data.start()
+
     barrier = pltpu.get_barrier_semaphore()
     for k in range(1, count):
         pl.semaphore_signal(barrier, inc=1, device_id=device(peer(k)), device_id_type=MESH)
     pl.semaphore_wait(barrier, count - 1)
 
-    halo = [
-        send(data_ref.at[:, pl.ds(width - VOXBLK, VOXBLK)], low_ref,
-             halo_send.at[0], halo_recv.at[0], peer(1)),
-        send(data_ref.at[:, pl.ds(0, VOXBLK)], high_ref,
-             halo_send.at[1], halo_recv.at[1], peer(count - 1)),
-    ]
-
+    load_maps.wait()
     maps = maps_ref[...]
     if gram_part.shape[0] > comps:
         gram_part[pl.ds(comps, gram_part.shape[0] - comps), :] = jnp.zeros(
@@ -135,6 +135,14 @@
     gram_copies = [
         send(gram_part.at[part(peer(k), gram_share, 8), :], gram_in.at[k], gsend.at[k], grecv.at[k], peer(k))
         for k in range(1, count)
+    ]
+
+    load_data.wait()
+    halo = [
+        send(data_ref.at[:, pl.ds(width - VOXBLK, VOXBLK)], low_ref,
+             halo_send.at[0], halo_recv.at[0], peer(1)),
+        send(data_ref.at[:, pl.ds(0, VOXBLK)], high_ref,
+             halo_send.at[1], halo_recv.at[1], peer(count - 1)),
     ]
 
     def columns(block):
@@ -208,6 +216,7 @@
     step = next(size for size in (40, 32, 24, 16, 8) if comps % size == 0)
     f32, bf16 = jnp.float32, jnp.bfloat16
     vmem = pl.BlockSpec(memory_space=pltpu.VMEM)
+    hbm = pl.BlockSpec(memory_space=pltpu.HBM)
     sems = pltpu.SemaphoreType.DMA((count,))
     return pl.pallas_call(
         functools.partial(kernel, count, sub_count, share, gram_share, step),
@@ -215,9 +224,12 @@
             jax.ShapeDtypeStruct((rows, width), bf16),
             jax.ShapeDtypeStruct((rows, comps), bf16),
         ),
-        in_specs=[vmem] * 4,
+        in_specs=[hbm, hbm, vmem, vmem],
         out_specs=(vmem, vmem),
         scratch_shapes=[
+            pltpu.VMEM((rows, width), bf16),
+            pltpu.VMEM((comps, width), bf16),
+            pltpu.SemaphoreType.DMA((2,)),
             pltpu.VMEM((rows, VOXBLK), bf16),
             pltpu.VMEM((rows, VOXBLK), bf16),
             pltpu.VMEM((count * gram_share, comps), f32),
@@ -232,7 +244,7 @@
             sems, sems, sems, sems, sems, sems, sems, sems,
         ],
         compiler_params=pltpu.CompilerParams(
-            collective_id=0, has_side_effects=True, vmem_limit_bytes=48 * 1024 * 1024
+            collective_id=0, has_side_effects=True, vmem_limit_bytes=60 * 1024 * 1024
         ),
     )(frames, maps, coef, keep)
 

time: 47.2 us -> 49.1 us (1.040)
  local copies, waits for them, and re-layouts: 2.86 us -> 0.17 us
  Pallas kernels: 39.8 us -> 41.8 us
  matrix products: 1.74 us -> 3.21 us
  other arithmetic: 2.4 us -> 3.7 us
    unnamed x6 -> x4, local copies, waits for them, and re-layouts: 2.86 us -> 0.17 us
    pallas_call x1, Pallas kernels: 39.8 us -> 41.8 us  [fused(): pl.pallas_call(functools.partial(kernel, count, sub_count, share, gram_sh...]
    dot_general x1, matrix products: 1.74 us -> 3.21 us  [local(): jnp.einsum('rc,cv->rv', beta, maps, preferred_element_type=jnp.float32)]
    another operation x1, other arithmetic: 0.04 us -> 0.66 us  [local(): jnp.stack([jnp.sum(jnp.where(offset == reach, slots, 0.0), axis=0) + (1.0...]
    reduce_max x1, other arithmetic: 0.74 us -> 1.32 us  [local(): jnp.max((labels == noise_labels[:, None]).astype(jnp.float32), axis=0, ke...]
where the time goes in v3:
time: 49.1 us; the launch traced here: 48.9 us
  Pallas kernels  41.8 us (85%)
  other arithmetic  3.7 us (8%)
  matrix products  3.21 us (7%)
    pallas_call x1, Pallas kernels, fused(): pl.pallas_call(functools.partial(kernel, count, sub_count, share, gram_sh...  41.8 us
    dot_general x1, matrix products, local(): jnp.einsum('rc,cv->rv', beta, maps, preferred_element_type=jnp.float32)  3.21 us
    reduce_max x1, other arithmetic, local(): jnp.max((labels == noise_labels[:, None]).astype(jnp.float32), axis=0, ke...  1.32 us
    reduce_sum x1, other arithmetic, local(): jnp.sum(jnp.where(offset == reach, slots, 0.0), axis=0)  1.02 us

profile of v3, /device:TPU:0, one launch (start us, length us, event | category | flops | bytes accessed | tf_op | source)
XLA Modules:
  0.0 48.9 jit_solution(16765482831399469364)
XLA Ops:
  0.0 1.3 %convert_reduce_fusion = f32[200]{0:T(256)} fusion(s32[64]{0:T(128)} %param.9), kind=kLoop, calls=%fused_computation.2 | loop fusion | flops 38200 | bytes 1056 | tf_op jit(solution)/shard_map/reduce_max | solution.py:291
  1.3 0.7 %compare_bitcast_fusion.1 = (pred[4,24]{1,0:T(4,128)(4,1)S(1)}, pred[4,24]{1,0:T(4,128)(4,1)S(1)}, pred[4,24]{1,0:T(4,128)(4,1)S(1)}) fusion(s32[24,4]{0,1:T(4,128)} %param.7, s32[24]{0:T(128)S(1)} %iota_add_fusion), kind=kLoop, calls=%fused_computation.13 | loop fusion | flops 384 | bytes 768 | tf_op jit(solution)/shard_map/eq | solution.py:286
  2.0 0.0 copy-start
  2.0 0.1 broadcast_bitcast_fusion.2
  2.1 0.1 broadcast_bitcast_fusion
  2.2 1.0 %select_reduce_fusion.2 = (f32[3072]{0:T(1024)S(1)}, f32[3072]{0:T(1024)S(1)}, f32[3072]{0:T(1024)S(1)}) fusion(f32[4,3072]{1,0:T(4,128)} %param.8, pred[1,4,24,128]{3,2,1,0:T(8,128)(4,1)S(1)} %broadcast_bitcast_fusion.2, pred[1,4,24,128]{3,2,1,0:T(8,128)(4,1)S(1)} %get-tuple-element.15, pred[1,4,24,128]{3,2,1,0:T(8,128)(4,1)S(1)} %get-tuple-element.16), kind=kLoop, calls=%fused_computation.7 | loop fusion | flops 64512 | bytes 122880 | tf_op jit(solution)/shard_map/reduce_sum | solution.py:286
  3.2 0.7 %pad_maximum_fusion.coef_ref = f32[3,3072]{1,0:T(4,128)} fusion(f32[1,3072]{1,0:T(1,128)S(1)} %bitcast.29, f32[1,3072]{1,0:T(1,128)S(1)} %bitcast.27, f32[1,3072]{1,0:T(1,128)S(1)} %bitcast.28), kind=kLoop, calls=%fused_computation.4 | loop fusion | flops 18432 | bytes 73728 | tf_op jit(solution)/shard_map/stack | solution.py:284
  3.9 41.8 %shard_map.55 = (bf16[256,3072]{1,0:T(8,128)(2,1)}, bf16[256,200]{1,0:T(8,128)(2,1)}) custom-call(bf16[256,3072]{1,0:T(8,128)(2,1)} %bitcast.26, bf16[200,3072]{1,0:T(8,128)(2,1)} %maps_hbm.1, f32[3,3072]{1,0:T(4,128)} %pad_maximum_fusion.coef_ref, f32[1,200]{1,0:T(1,128)} %bitcast.30), custom_call_target="tpu_custom_call" | custom-call | tf_op jit(solution)/shard_map/pallas_call | solution.py:221
  45.7 0.0 copy-done
  45.7 3.2 %fusion = bf16[256,3072]{1,0:T(8,128)(2,1)} fusion(bf16[256,200]{1,0:T(8,128)(2,1)} %get-tuple-element.8, bf16[200,3072]{1,0:T(8,128)(2,1)S(1)} %copy-done, bf16[256,3072]{1,0:T(8,128)(2,1)} %get-tuple-element.7), kind=kOutput, calls=%fused_computation.1 | convolution fusion | flops 316932096 | bytes 4476928 | tf_op jit(solution)/shard_map/rc,cv->rv/dot_general | solution.py:297
  (2 shorter events, 0.0 us)
Async XLA Ops:
  2.0 43.7 %copy-start = (bf16[200,3072]{1,0:T(8,128)(2,1)S(1)}, bf16[200,3072]{1,0:T(8,128)(2,1)}, u32[]{:S(2)}) copy-start(bf16[200,3072]{1,0:T(8,128)(2,1)} %maps_hbm.1) | copy-start | bytes 3686404

commit v4 on v2

--- a/solution.py
+++ b/solution.py
@@ -88,8 +88,9 @@
 
 def kernel(
     count, sub_count, share, gram_share, step,
-    data_ref, maps_ref, coef_ref, keep_ref,
+    data_ref, maps_ref, neighbour_ref, weight_ref, label_ref,
     smooth_ref, beta_ref,
+    pick_ref,
     low_ref, high_ref, gram_part, gram_in, gram_all, proj_part, proj_in, work_ref, beta_all,
     halo_send, halo_recv, gsend, grecv, asend, arecv, psend, precv, bsend, brecv,
 ):
@@ -137,15 +138,35 @@
         for k in range(1, count)
     ]
 
+    slots = weight_ref.shape[0]
+    own_block = me * blocks + lax.broadcasted_iota(jnp.int32, (blocks, VOXBLK), 0)
+    for slot in range(slots):
+        offset = jnp.broadcast_to(neighbour_ref[:, slot : slot + 1], (blocks, VOXBLK)) - own_block
+        for reach in range(-NEIGHBOUR_REACH, NEIGHBOUR_REACH + 1):
+            pick_ref[(reach + NEIGHBOUR_REACH) * slots + slot] = (offset == reach).astype(jnp.float32)
+    comp_id = lax.broadcasted_iota(jnp.int32, (comps, label_ref.shape[1]), 0)
+    hit = jnp.max((comp_id == label_ref[...]).astype(jnp.float32), axis=1, keepdims=True)
+    diagonal = lax.broadcasted_iota(jnp.int32, (comps, comps), 0) == lax.broadcasted_iota(
+        jnp.int32, (comps, comps), 1
+    )
+    keep = jnp.sum(jnp.where(diagonal, hit, 0.0), axis=0, keepdims=True)
+
     def columns(block):
         start = block * VOXBLK
         return pl.ds(start if isinstance(block, int) else pl.multiple_of(start, VOXBLK), VOXBLK)
 
     def smooth(block, low, high):
         here = columns(block)
-        weight = coef_ref[:, here]
-        total = data_ref[:, here].astype(jnp.float32) * weight[1:2]
-        total = total + low.astype(jnp.float32) * weight[0:1] + high.astype(jnp.float32) * weight[2:3]
+
+        def weight(reach):
+            place = (reach + NEIGHBOUR_REACH) * slots
+            return sum(
+                weight_ref[pl.ds(slot, 1), here] * pick_ref[place + slot, pl.ds(block, 1), :]
+                for slot in range(slots)
+            )
+
+        total = data_ref[:, here].astype(jnp.float32) * (weight(0) + 1.0)
+        total = total + low.astype(jnp.float32) * weight(-1) + high.astype(jnp.float32) * weight(1)
         smooth_ref[:, here] = total.astype(jnp.bfloat16)
 
     def inner(block, carry):
@@ -190,7 +211,7 @@
     beta = -f32_dot(rhs, work_ref[...], NN)
     left = rhs - f32_dot(beta, gram, NN)
     beta = beta - f32_dot(left, work_ref[...], NN)
-    beta_all[mine, :] = jnp.where(keep_ref[...] > 0.0, beta, 0.0).astype(jnp.bfloat16)
+    beta_all[mine, :] = jnp.where(keep > 0.0, beta, 0.0).astype(jnp.bfloat16)
     beta_copies = [
         send(beta_all.at[mine, :], beta_all.at[mine, :], bsend.at[k], brecv.at[k], peer(k))
         for k in range(1, count)
@@ -200,7 +221,7 @@
     beta_ref[...] = beta_all[...]
 
 
-def fused(frames, maps, coef, keep, count, sub_count):
+def fused(frames, maps, neighbours, weights, labels, count, sub_count):
     rows, width = frames.shape
     comps = maps.shape[0]
     share = rows // count
@@ -215,9 +236,10 @@
             jax.ShapeDtypeStruct((rows, width), bf16),
             jax.ShapeDtypeStruct((rows, comps), bf16),
         ),
-        in_specs=[vmem] * 4,
+        in_specs=[vmem] * 5,
         out_specs=(vmem, vmem),
         scratch_shapes=[
+            pltpu.VMEM(((2 * NEIGHBOUR_REACH + 1) * weights.shape[0], width // VOXBLK, VOXBLK), f32),
             pltpu.VMEM((rows, VOXBLK), bf16),
             pltpu.VMEM((rows, VOXBLK), bf16),
             pltpu.VMEM((count * gram_share, comps), f32),
@@ -234,7 +256,7 @@
         compiler_params=pltpu.CompilerParams(
             collective_id=0, has_side_effects=True, vmem_limit_bytes=48 * 1024 * 1024
         ),
-    )(frames, maps, coef, keep)
+    )(frames, maps, neighbours, weights, labels)
 
 
 def solve_gram(gram, rhs):
@@ -266,21 +288,23 @@
     rows = subjects * frames
     sub_count = lax.axis_size("sub")
     count = lax.axis_size("vox") * sub_count
-    own = lax.axis_index(("vox", "sub")) * blocks + jnp.arange(blocks, dtype=jnp.int32)
-    offset = (neighbours - own[:, None]).T[:, :, None]
-    slots = weights.reshape(weights.shape[0], blocks, VOXBLK)
-    coef = jnp.stack(
-        [
-            jnp.sum(jnp.where(offset == reach, slots, 0.0), axis=0) + (1.0 if reach == 0 else 0.0)
-            for reach in range(-NEIGHBOUR_REACH, NEIGHBOUR_REACH + 1)
-        ]
-    ).reshape(2 * NEIGHBOUR_REACH + 1, width)
-    labels = lax.broadcasted_iota(jnp.int32, (noise_labels.shape[0], comps), 1)
-    keep = jnp.max((labels == noise_labels[:, None]).astype(jnp.float32), axis=0, keepdims=True)
     stacked = data.reshape(rows, width)
     if rows % (16 * count) == 0 and count <= 16 and blocks > 2:
-        smoothed, beta = fused(stacked, maps, coef, keep, count, sub_count)
+        smoothed, beta = fused(
+            stacked, maps, neighbours, weights, noise_labels.reshape(1, -1), count, sub_count
+        )
     else:
+        own = lax.axis_index(("vox", "sub")) * blocks + jnp.arange(blocks, dtype=jnp.int32)
+        offset = (neighbours - own[:, None]).T[:, :, None]
+        slots = weights.reshape(weights.shape[0], blocks, VOXBLK)
+        coef = jnp.stack(
+            [
+                jnp.sum(jnp.where(offset == reach, slots, 0.0), axis=0) + (1.0 if reach == 0 else 0.0)
+                for reach in range(-NEIGHBOUR_REACH, NEIGHBOUR_REACH + 1)
+            ]
+        ).reshape(2 * NEIGHBOUR_REACH + 1, width)
+        labels = lax.broadcasted_iota(jnp.int32, (noise_labels.shape[0], comps), 1)
+        keep = jnp.max((labels == noise_labels[:, None]).astype(jnp.float32), axis=0, keepdims=True)
         smoothed, beta = by_collectives(stacked, maps, coef, keep, count)
     fitted = jnp.einsum("rc,cv->rv", beta, maps, preferred_element_type=jnp.float32)
     clean = (smoothed.astype(jnp.float32) - fitted).astype(jnp.bfloat16)

time: 47.2 us -> 46.7 us (0.989)
  other arithmetic: 2.4 us -> 0 us
  local copies, waits for them, and re-layouts: 2.86 us -> 4.91 us
    unnamed x6 -> x9, local copies, waits for them, and re-layouts: 2.86 us -> 4.91 us
    reduce_sum x1 -> x0, other arithmetic: 0.92 us -> none  [local(): jnp.sum(jnp.where(offset == reach, slots, 0.0), axis=0)]
    reduce_max x1 -> x0, other arithmetic: 0.74 us -> none  [local(): jnp.max((labels == noise_labels[:, None]).astype(jnp.float32), axis=0, ke...]
    eq x1 -> x0, other arithmetic: 0.69 us -> none  [local(): offset == reach]
where the time goes in v4:
time: 46.7 us; the launch traced here: 46.5 us
  Pallas kernels  39.8 us (85%)
  local copies, waits for them, and re-layouts  4.91 us (11%)
  matrix products  1.72 us (4%)
    pallas_call x1, Pallas kernels, fused(): pl.pallas_call(functools.partial(kernel, count, sub_count, share, gram_sh...  39.8 us
    unnamed x9, local copies, waits for them, and re-layouts  4.91 us
    dot_general x1, matrix products, local(): jnp.einsum('rc,cv->rv', beta, maps, preferred_element_type=jnp.float32)  1.72 us

profile of v4, /device:TPU:0, one launch (start us, length us, event | category | flops | bytes accessed | tf_op | source)
XLA Modules:
  0.0 46.5 jit_solution(6481161836369198967)
XLA Ops:
  0.0 0.8 %copy.6.neighbour_ref = s32[24,4]{1,0:T(8,128)S(1)} copy(s32[24,4]{0,1:T(4,128)} %param.7) | data formatting | bytes 768 | tf_op args[2]
  0.8 0.0 copy-start
  0.8 1.3 %copy-done = bf16[200,3072]{1,0:T(8,128)(2,1)S(1)} copy-done((bf16[200,3072]{1,0:T(8,128)(2,1)S(1)}, bf16[200,3072]{1,0:T(8,128)(2,1)}, u32[]{:S(2)}) %copy-start) | copy-done | bytes 1228824
  2.0 0.0 copy-start.1
  2.1 1.4 %copy-done.1 = bf16[2,128,3072]{2,1,0:T(8,128)(2,1)S(1)} copy-done((bf16[2,128,3072]{2,1,0:T(8,128)(2,1)S(1)}, bf16[2,128,3072]{2,1,0:T(8,128)(2,1)}, u32[]{:S(2)}) %copy-start.1) | copy-done | bytes 1572888
  3.5 0.0 copy-start.2
  3.5 0.8 %copy-done.2 = f32[4,3072]{1,0:T(4,128)S(1)} copy-done((f32[4,3072]{1,0:T(4,128)S(1)}, f32[4,3072]{1,0:T(4,128)}, u32[]{:S(2)}) %copy-start.2) | copy-done | bytes 49176
  4.3 0.0 copy-start.3
  4.3 0.7 %copy-done.3 = s32[64]{0:T(128)S(1)} copy-done((s32[64]{0:T(128)S(1)}, s32[64]{0:T(128)}, u32[]{:S(2)}) %copy-start.3) | copy-done | bytes 280
  4.9 39.8 %shard_map.55 = (bf16[256,3072]{1,0:T(8,128)(2,1)S(1)}, bf16[256,200]{1,0:T(8,128)(2,1)S(1)}) custom-call(bf16[256,3072]{1,0:T(8,128)(2,1)S(1)} %bitcast.5, bf16[200,3072]{1,0:T(8,128)(2,1)S(1)} %copy-done, s32[24,4]{1,0:T(8,128)S(1)} %copy.6.neighbour_ref, f32[4,3072]{1,0:T(4,128)S(1)} %copy-done.2, s32[1,64]{1,0:T(1,128)S(1)} %bitcast.6), custom_call_target="tpu_custom_call" | custom-call | tf_op jit(solution)/shard_map/pallas_call | solution.py:233
  44.8 1.7 %fusion = bf16[256,3072]{1,0:T(8,128)(2,1)} fusion(bf16[256,200]{1,0:T(8,128)(2,1)S(1)} %get-tuple-element.8, bf16[200,3072]{1,0:T(8,128)(2,1)S(1)} %copy-done, bf16[256,3072]{1,0:T(8,128)(2,1)S(1)} %get-tuple-element.7), kind=kOutput, calls=%fused_computation.1 | convolution fusion | flops 316932096 | bytes 4476928 | tf_op jit(solution)/shard_map/rc,cv->rv/dot_general | solution.py:309
Async XLA Ops:
  0.8 1.3 %copy-start = (bf16[200,3072]{1,0:T(8,128)(2,1)S(1)}, bf16[200,3072]{1,0:T(8,128)(2,1)}, u32[]{:S(2)}) copy-start(bf16[200,3072]{1,0:T(8,128)(2,1)} %maps_ref.1) | copy-start | bytes 3686404
  2.0 1.4 %copy-start.1 = (bf16[2,128,3072]{2,1,0:T(8,128)(2,1)S(1)}, bf16[2,128,3072]{2,1,0:T(8,128)(2,1)}, u32[]{:S(2)}) copy-start(bf16[2,128,3072]{2,1,0:T(8,128)(2,1)} %param.5) | copy-start | bytes 4718596
  3.5 0.8 %copy-start.2 = (f32[4,3072]{1,0:T(4,128)S(1)}, f32[4,3072]{1,0:T(4,128)}, u32[]{:S(2)}) copy-start(f32[4,3072]{1,0:T(4,128)} %weight_ref.1) | copy-start | bytes 147460
  4.3 0.7 %copy-start.3 = (s32[64]{0:T(128)S(1)}, s32[64]{0:T(128)}, u32[]{:S(2)}) copy-start(s32[64]{0:T(128)} %param.9) | copy-start | bytes 772
